TPU v7x, 32 devices: a whole 2x2x4 slice. The times are simulated.
32 devices in a mesh: grp: 2 (over y), param: 16 (over z, x, core).
Axes of the slice: x: 2, y: 2, z: 4, core: 2. Of those that a mesh axis runs over, the one named last changes fastest.
Arguments:
- basis_a: bfloat16 [8192, 8192], P('param'), may hold values from -0.0625 to 0.0625
- basis_g: bfloat16 [14336, 14336], P('param'), may hold values from -0.046875 to 0.046875
- query_a: bfloat16 [16, 32, 8192], P('grp', None, 'param'), parts along dimension 0, may hold values from -0.0625 to 0.0625
- query_g: bfloat16 [16, 32, 14336], P('grp', None, 'param'), parts along dimension 0, may hold values from -0.046875 to 0.046875
- acts: bfloat16 [6144, 8192], P(('grp', 'param')), parts along dimension 0, may hold values from -6 to 6
- grads: bfloat16 [6144, 14336], P(('grp', 'param')), parts along dimension 0, may hold values from -0.29882812 to 0.29882812
- cand_blocks: int32 [8, 4], P('grp'), parts along dimension 0, may hold values from 0 to 15, as said below
- cand_count: int32 [8], P('grp'), parts along dimension 0, may hold values from 1 to 4, as said below
Outputs:
- scores: float32 [16, 48], P('grp', 'param'), parts along dimension 0
- top_scores: float32 [16, 16], P('grp'), parts along dimension 0
There are 2 independent parts, one for each index of `grp`. A program takes and returns all parts, laid end to end along the dimension named above; an argument that names none is the same for every part. Nothing has to cross between parts.
Inputs may be any that keep to these rules, and one draw needn't show every extreme that they name: `cand_blocks`: within a row the ids are distinct. Counting only the first cand_count slots of each row, every sequence block is listed by at most 2 query blocks, and some block by exactly 2. `cand_count`: some query block uses all 4 slots.
All inputs are finite; a program needn't handle non-finite values.
Results may differ from a plain program's by a relative error of at most 0.0045.
Values may be sent and summed in bfloat16 or wider, within the bound.
A program may use at most 192 MiB of HBM per device.

v0:
```python
import jax
import jax.numpy as jnp
from jax import lax
from jax.sharding import PartitionSpec as P

SEQ_LEN = 64
TOPK = 16


def merged(part, axis, combine):
    gathered = lax.all_gather(part, axis)

    def take(source):
        return lax.dynamic_index_in_dim(gathered, source, 0, False)

    return lax.fori_loop(
        1, lax.axis_size(axis), lambda source, state: combine(state, take(source)), take(0)
    )


def contract_last(left, right):
    return lax.dot_general(
        left, right, (((1,), (1,)), ((), ())), preferred_element_type=jnp.float32
    )


def top_values(first_set, second_set):
    return lax.top_k(jnp.concatenate([first_set, second_set], axis=1), TOPK)[0]


def shards(basis_a, basis_g, query_a, query_g, acts, grads, cand_blocks, cand_count):
    width_a = basis_a.shape[0]
    width_g = basis_g.shape[0]
    stride = width_a + width_g
    queries = query_a.shape[0]
    rank_size = query_a.shape[1]
    rows_qr = queries * rank_size
    tok_rows = acts.shape[0]
    seq_count = tok_rows // SEQ_LEN
    blocks_q = cand_blocks.shape[0]
    per_block = queries // blocks_q
    my_index = lax.axis_index("param")
    joined = jnp.concatenate([query_a, query_g], axis=2)
    piece = lax.all_gather(joined, "param", axis=2, tiled=True)
    shard_count = piece.shape[2] // stride
    divided = piece.reshape(rows_qr, shard_count, stride)
    part_a = divided[:, :, :width_a].reshape(rows_qr, shard_count * width_a)
    part_g = divided[:, :, width_a:].reshape(rows_qr, shard_count * width_g)
    back_a = contract_last(part_a, basis_a)
    back_g = contract_last(part_g, basis_g)
    back_joined = jnp.concatenate(
        [back_a.astype(jnp.bfloat16), back_g.astype(jnp.bfloat16)], axis=1
    )
    positions = jnp.arange(cand_blocks.shape[1], dtype=jnp.int32)
    live_slot = positions[None, :] < cand_count[:, None]
    piece = lax.all_gather(back_joined, "param", axis=1, tiled=True)
    shard_count = piece.shape[1] // stride
    divided = piece.reshape(rows_qr, shard_count, stride)
    part_a = divided[:, :, :width_a].reshape(rows_qr, shard_count * width_a)
    part_g = divided[:, :, width_a:].reshape(rows_qr, shard_count * width_g)
    proj_a = contract_last(part_a, acts)
    proj_g = contract_last(part_g, grads)
    token_sums = (proj_a * proj_g).reshape(queries, rank_size, tok_rows).sum(axis=1)
    seq_sums = token_sums.reshape(queries, seq_count, SEQ_LEN).sum(axis=2)
    named_here = jnp.sum((live_slot & (cand_blocks == my_index)).astype(jnp.float32), axis=1)
    masking = jnp.repeat(named_here, per_block)
    scores = seq_sums * masking[:, None]
    padded = jnp.concatenate([scores, jnp.full((queries, TOPK), -1e30, jnp.float32)], axis=1)
    local_top = lax.top_k(padded, TOPK)[0]
    top_scores = merged(local_top, "param", top_values)
    return (scores, top_scores)


def solution(mesh):
    in_specs = (
        P("param", None),
        P("param", None),
        P("grp", None, "param"),
        P("grp", None, "param"),
        P(("grp", "param"), None),
        P(("grp", "param"), None),
        P("grp", None),
        P("grp"),
    )
    out_specs = (P("grp", "param"), P("grp", None))
    return jax.shard_map(shards, mesh=mesh, in_specs=in_specs, out_specs=out_specs, check_vma=False)
```

profile of v0, /device:TPU:0, one launch (start us, length us, event | category | flops | bytes accessed | tf_op | source)
XLA Modules:
  0.0 340.1 jit_solution(5697549203394737251)
XLA Ops:
  7.2 2.2 pad_maximum_fusion.1
  9.5 97.5 %all-gather.4.cloned.1.call-done = bf16[8,32,22528]{2,1,0:T(8,128)(2,1)} async-done(((bf16[8,32,1408]{2,1,0:T(8,128)(2,1)}), bf16[8,32,22528]{2,1,0:T(8,128)(2,1)}) %all-gather.4.cloned.1.call-update) | async-done | bytes 11534352 | tf_op jit(solution)/shard_map/all_gather | solution.py:44
  106.9 7.6 %copy.27 = bf16[32,8,16,1408]{3,2,1,0:T(8,128)(2,1)S(1)} copy(bf16[32,8,16,1408]{3,1,2,0:T(8,128)(2,1)} %bitcast.39) | data formatting | bytes 23068672
  114.6 4.3 %copy-done.1 = bf16[32,8,16,1408]{3,2,1,0:T(8,128)(2,1)} copy-done((bf16[32,8,16,1408]{3,2,1,0:T(8,128)(2,1)}, bf16[32,8,16,1408]{3,2,1,0:T(8,128)(2,1)S(1)}, u32[]{:S(2)}) %copy-start.1) | copy-done | bytes 11534360
  118.9 2.6 slice.27
  121.6 3.7 %slice.28 = bf16[256,16,896]{2,1,0:T(8,128)(2,1)S(1)} slice(bf16[256,16,1408]{2,1,0:T(8,128)(2,1)} %bitcast.30), slice={[0:256], [0:16], [512:1408]} | slice | bytes 14680064 | tf_op jit(solution)/shard_map/slice | solution.py:48
  125.2 5.2 %copy.29 = bf16[32,8,16,896]{3,1,2,0:T(8,128)(2,1)} copy(bf16[32,8,16,896]{3,2,1,0:T(8,128)(2,1)S(1)} %bitcast.33) | data formatting | bytes 14680064
  130.5 8.6 %copy.28 = bf16[32,8,16,512]{3,1,2,0:T(8,128)(2,1)} copy(bf16[32,8,16,512]{3,2,1,0:T(8,128)(2,1)} %bitcast.36) | data formatting | bytes 8388608
  139.0 15.3 %convolution_convert_fusion = bf16[256,896]{1,0:T(8,128)(2,1)} fusion(bf16[256,14336]{1,0:T(8,128)(2,1)} %bitcast.40, bf16[896,14336]{1,0:T(8,128)(2,1)} %param.11), kind=kOutput, calls=%fused_computation.2 | convolution fusion | flops 6576898048 | bytes 33488896 | tf_op jit(solution)/shard_map/dot_general | solution.py:22
  154.3 7.1 %convolution_convert_fusion.1 = bf16[256,512]{1,0:T(8,128)(2,1)S(1)} fusion(bf16[256,8192]{1,0:T(8,128)(2,1)} %bitcast.41, bf16[512,8192]{1,0:T(8,128)(2,1)} %param.10), kind=kOutput, calls=%fused_computation.3 | convolution fusion | flops 2147614720 | bytes 12845056 | tf_op jit(solution)/shard_map/dot_general | solution.py:22
  161.4 0.9 pad_maximum_fusion.2
  162.7 92.1 %all-gather.6.cloned.1.call-done = bf16[256,22528]{1,0:T(8,128)(2,1)} async-done(((bf16[256,1408]{1,0:T(8,128)(2,1)}), bf16[256,22528]{1,0:T(8,128)(2,1)}) %all-gather.6.cloned.1.call-update) | async-done | bytes 11534352 | tf_op jit(solution)/shard_map/all_gather | solution.py:56
  254.8 7.6 %copy.30 = bf16[32,8,16,1408]{3,2,1,0:T(8,128)(2,1)S(1)} copy(bf16[32,8,16,1408]{3,1,2,0:T(8,128)(2,1)} %bitcast.38) | data formatting | bytes 23068672
  262.5 4.3 %copy-done.2 = bf16[32,8,16,1408]{3,2,1,0:T(8,128)(2,1)} copy-done((bf16[32,8,16,1408]{3,2,1,0:T(8,128)(2,1)}, bf16[32,8,16,1408]{3,2,1,0:T(8,128)(2,1)S(1)}, u32[]{:S(2)}) %copy-start.2) | copy-done | bytes 11534360
  266.8 2.6 slice.29
  269.4 6.7 %slice.30 = bf16[256,16,896]{2,1,0:T(8,128)(2,1)} slice(bf16[256,16,1408]{2,1,0:T(8,128)(2,1)} %bitcast.32), slice={[0:256], [0:16], [512:1408]} | slice | bytes 14680064 | tf_op jit(solution)/shard_map/slice | solution.py:60
  276.1 5.3 %copy.32 = bf16[32,8,16,896]{3,1,2,0:T(8,128)(2,1)S(1)} copy(bf16[32,8,16,896]{3,2,1,0:T(8,128)(2,1)} %bitcast.34) | data formatting | bytes 14680064
  281.4 6.5 %copy.31 = bf16[32,8,16,512]{3,1,2,0:T(8,128)(2,1)S(1)} copy(bf16[32,8,16,512]{3,2,1,0:T(8,128)(2,1)} %bitcast.37) | data formatting | bytes 8388608
  287.9 1.5 fusion.1
  289.5 5.8 %convolution_multiply_fusion = f32[256,192]{0,1:T(8,128)} fusion(f32[256,192]{0,1:T(8,128)S(1)} %fusion.1, bf16[256,14336]{1,0:T(8,128)(2,1)S(1)} %bitcast.28, bf16[192,14336]{1,0:T(8,128)(2,1)} %param.15), kind=kOutput, calls=%fused_computation.4 | convolution fusion | flops 1409335296 | bytes 13238272 | tf_op jit(solution)/shard_map/dot_general | solution.py:22
  295.3 1.1 copy.20
  297.6 18.8 %all-gather = f32[128,16]{1,0:T(8,128)S(1)} all-gather(f32[8,16]{1,0:T(8,128)S(1)} %copy.22), channel_id=2, replica_groups=mesh['grp'=2,'param'=16] {'param'}, dimensions={0}, use_global_device_ids=true | all-gather | bytes 8704 | tf_op jit(solution)/shard_map/all_gather | solution.py:11
  316.5 16.0 %while.15 = (s32[]{:T(128)}, f32[8,16]{0,1:T(8,128)S(1)}, f32[16,8,16]{2,1,0:T(8,128)S(1)}, s32[]{:T(128)}, s32[]{:T(128)}, /*index=5*/s32[]{:T(128)}) while((s32[]{:T(128)}, f32[8,16]{0,1:T(8,128)S(1)}, f32[16,8,16]{2,1,0:T(8,128)S(1)}, s32[]{:T(128)}, s32[]{:T(128)}, /*index=5*/s32[]{:T(128)}) %tuple.52), condition=%wide.region_6.7_spmd, body=%wide.region_4.0_spmd.sunk | while | flops 2309 | bytes 12395 | solution.py:16
  316.8 0.8 top_k.22
  320.0 0.8 top_k.22
  321.0 0.8 top_k.22
  323.2 0.8 top_k.22
  324.2 0.8 top_k.22
  325.3 0.8 top_k.22
  327.4 0.8 top_k.22
  328.5 0.8 top_k.22
  329.6 0.8 top_k.22
  (128 shorter events, 11.0 us)
Async XLA Ops:
  7.2 280.8 %copy-start = (bf16[192,8192]{1,0:T(8,128)(2,1)S(1)}, bf16[192,8192]{1,0:T(8,128)(2,1)}, u32[]{:S(2)}) copy-start(bf16[192,8192]{1,0:T(8,128)(2,1)} %param.14) | copy-start | bytes 9437188
  7.2 99.8 %all-gather.4.cloned.1.call-start = ((), (), s32[]{:S(2)}) async-start(), calls=%async_computation | async-start | bytes 12255232 | tf_op jit(solution)/shard_map/all_gather | solution.py:44
  9.4 245.4 %all-gather.6.cloned.1.call-start = ((), (), s32[]{:S(2)}) async-start(), calls=%async_computation.1 | async-start | bytes 12255232 | tf_op jit(solution)/shard_map/all_gather | solution.py:56
  114.6 4.4 %copy-start.1 = (bf16[32,8,16,1408]{3,2,1,0:T(8,128)(2,1)}, bf16[32,8,16,1408]{3,2,1,0:T(8,128)(2,1)S(1)}, u32[]{:S(2)}) copy-start(bf16[32,8,16,1408]{3,2,1,0:T(8,128)(2,1)S(1)} %copy.27) | copy-start | bytes 34603012
  154.3 7.1 %copy-start.3 = (bf16[256,896]{1,0:T(8,128)(2,1)S(1)}, bf16[256,896]{1,0:T(8,128)(2,1)}, u32[]{:S(2)}) copy-start(bf16[256,896]{1,0:T(8,128)(2,1)} %convolution_convert_fusion) | copy-start | bytes 1376260
  154.3 8.0 %copy-start.5 = (s32[4,4]{1,0:T(4,128)S(1)}, s32[4,4]{1,0:T(4,128)}, u32[]{:S(2)}) copy-start(s32[4,4]{1,0:T(4,128)} %param.16) | copy-start | bytes 196
  154.3 8.0 %copy-start.6 = (s32[4]{0:T(128)S(1)}, s32[4]{0:T(128)}, u32[]{:S(2)}) copy-start(s32[4]{0:T(128)} %param.17) | copy-start | bytes 52
  262.5 4.4 %copy-start.2 = (bf16[32,8,16,1408]{3,2,1,0:T(8,128)(2,1)}, bf16[32,8,16,1408]{3,2,1,0:T(8,128)(2,1)S(1)}, u32[]{:S(2)}) copy-start(bf16[32,8,16,1408]{3,2,1,0:T(8,128)(2,1)S(1)} %copy.30) | copy-start | bytes 34603012
  296.7 36.5 %copy-start.4 = (f32[8,3]{0,1:T(4,128)}, f32[8,3]{0,1:T(4,128)S(1)}, u32[]{:S(2)}) copy-start(f32[8,3]{0,1:T(4,128)S(1)} %copy.24) | copy-start | bytes 292
Sparse Core Ops, SparseCore 0:
  10.2 96.6 all-gather.3
  162.4 92.3 all-gather.5
where the time goes:
time: 341 us; the launch traced here: 340 us
  waiting for transfers between devices  190 us (56%)
  local copies, waits for them, and re-layouts  69.7 us (20%)
  matrix products  29.7 us (9%)
  blocking collectives  18.8 us (6%)
  other arithmetic  17.9 us (5%)
  between operations  14.2 us (4%)
    all_gather x1, waiting for transfers between devices, shards(): piece = lax.all_gather(joined, 'param', axis=2, tiled=True)  97.5 us
    all_gather x1, waiting for transfers between devices, shards(): piece = lax.all_gather(back_joined, 'param', axis=1, tiled=True)  92.1 us
    unnamed x22, local copies, waits for them, and re-layouts  50.3 us
    dot_general x4, matrix products, contract_last(): lax.dot_general(left, right, (((1,), (1,)), ((), ())), preferred_element_...  29.7 us
    all_gather x1, blocking collectives, merged(): gathered = lax.all_gather(part, axis)  18.8 us
    top_k x15, other arithmetic, top_values(): return lax.top_k(jnp.concatenate([first_set, second_set], axis=1), TOPK)[0]  12.5 us
    slice x2, local copies, waits for them, and re-layouts, shards(): part_g = divided[:, :, width_a:].reshape(rows_qr, shard_count * width_g)  10.3 us
  transfers between devices with their start and end apart: 2, of which 2 were waited for; matrix products, arithmetic and copies ran while one was open for 0% of the time, Pallas kernels for 0%

commit v1 on v0

v1 whole, which is shorter than its diff:
```python
import functools

import jax
import jax.numpy as jnp
from jax import lax
from jax.experimental import pallas as pl
from jax.experimental.pallas import tpu as pltpu
from jax.sharding import PartitionSpec as P

SEQ_LEN = 64
TOPK = 16
CORES = 2
X_CHIPS = 2
BASIS_SLOTS = 4
LANES = 128


def contract_last(left, right):
    return lax.dot_general(
        left, right, (((1,), (1,)), ((), ())), preferred_element_type=jnp.float32
    )


def ring_kernel(
    n, qa_ref, qg_ref, ba_ref, bg_ref, acts_ref, grads_ref, cand_ref, count_ref,
    scores_ref, top_ref,
    qbuf, bbuf, slot_a, slot_g, acts_v, grads_v, acc_a, acc_g, proj_a, proj_g, seq_all,
    own_sem, basis_sem, token_sem,
    right_sem, left_sem, pair_sem, land_sem, score_send, score_land,
):
    rows, width_a = qa_ref.shape
    width_g = qg_ref.shape[1]
    half = rows // 2
    chips = n // CORES
    z_chips = chips // X_CHIPS
    reach = chips // 2
    me = lax.axis_index("param")
    core = lax.rem(me, CORES)
    chip = lax.div(me, CORES)
    x_pos = lax.rem(chip, X_CHIPS)
    z_pos = lax.div(chip, X_CHIPS)
    pos = z_pos + x_pos * (chips - 1 - 2 * z_pos)
    pair = me + 1 - 2 * core

    def holder(place, which):
        place = lax.rem(place + 2 * chips, chips)
        x = lax.div(place, z_chips)
        z = place + x * (chips - 1 - 2 * place)
        return (z * X_CHIPS + x) * CORES + which

    right = holder(pos + 1, core)
    left = holder(pos - 1, core)

    def source(j):
        turn = j + 2
        k = lax.div(turn, 4)
        t = lax.rem(turn, 4)
        flip = lax.rem(t, 2)
        side = lax.div(t, 2)
        return holder(pos - k + 2 * k * side, core + flip * (1 - 2 * core))

    def basis_copies(j):
        s = source(j)
        place = lax.rem(j, BASIS_SLOTS)
        cols_a = pl.ds(pl.multiple_of(s * width_a, LANES), width_a)
        cols_g = pl.ds(pl.multiple_of(s * width_g, LANES), width_g)
        return (
            pltpu.make_async_copy(ba_ref.at[:, cols_a], slot_a.at[place], basis_sem.at[0, place]),
            pltpu.make_async_copy(bg_ref.at[:, cols_g], slot_g.at[place], basis_sem.at[1, place]),
        )

    own = (
        pltpu.make_async_copy(qa_ref, qbuf.at[me, :, pl.ds(0, width_a)], own_sem.at[0]),
        pltpu.make_async_copy(qg_ref, qbuf.at[me, :, pl.ds(width_a, width_g)], own_sem.at[1]),
    )
    tokens = (
        pltpu.make_async_copy(acts_ref, acts_v, token_sem.at[0]),
        pltpu.make_async_copy(grads_ref, grads_v, token_sem.at[1]),
    )
    for copy in own:
        copy.start()
    for j in range(BASIS_SLOTS):
        for copy in basis_copies(jnp.int32(j)):
            copy.start()
    for copy in tokens:
        copy.start()

    barrier = pltpu.get_barrier_semaphore()

    def greet(j, carry):
        pl.semaphore_signal(
            barrier, inc=1, device_id={"param": lax.rem(me + j, n)},
            device_id_type=pl.DeviceIdType.MESH,
        )
        return carry

    lax.fori_loop(1, n, greet, 0)
    acc_a[...] = jnp.zeros_like(acc_a)
    acc_g[...] = jnp.zeros_like(acc_g)
    proj_a[...] = jnp.zeros_like(proj_a)
    proj_g[...] = jnp.zeros_like(proj_g)
    pl.semaphore_wait(barrier, n - 1)
    for copy in own:
        copy.wait()

    def stage(number, buf, compute):
        sent = []

        def push(s, h, target, sem):
            view = buf.at[s, pl.ds(h * half, half), :]
            return pltpu.make_async_remote_copy(
                src_ref=view, dst_ref=view, send_sem=sem, recv_sem=land_sem.at[number, s, h],
                device_id={"param": target}, device_id_type=pl.DeviceIdType.MESH,
            )

        def send(s, h, target, sem):
            copy = push(s, h, target, sem)
            copy.start()
            sent.append(copy)

        def landed(s, h):
            push(s, h, pair, pair_sem.at[number, 0, 0, h]).wait_recv()

        for h in (0, 1):
            send(me, h, right, right_sem.at[number, 0, h])
            send(me, 1 - h, left, left_sem.at[number, 0, 1 - h])
        for h in (0, 1):
            send(me, h, pair, pair_sem.at[number, 0, 0, h])
        compute(0)
        for h in (0, 1):
            landed(pair, h)
        compute(1)
        for k in range(1, reach):
            back, front = holder(pos - k, core), holder(pos + k, core)
            for h in (0, 1):
                landed(back, h)
                if k < reach - 1 or h == 0:
                    send(back, h, right, right_sem.at[number, k, h])
                landed(front, 1 - h)
                if k < reach - 1 or h == 0:
                    send(front, 1 - h, left, left_sem.at[number, k, 1 - h])
                send(back, h, pair, pair_sem.at[number, 0, k, h])
                send(front, 1 - h, pair, pair_sem.at[number, 1, k, 1 - h])
            for other in (holder(pos - k, 1 - core), holder(pos + k, 1 - core)):
                for h in (0, 1):
                    landed(other, h)

            def body(j, carry):
                compute(j)
                return carry

            lax.fori_loop(4 * k - 2, 4 * k + 2, body, 0)
        far = holder(pos - reach, core)
        for h in (0, 1):
            landed(far, h)
            send(far, h, pair, pair_sem.at[number, 0, reach, h])
        compute(n - 2)
        for h in (0, 1):
            landed(holder(pos - reach, 1 - core), h)
        compute(n - 1)
        return sent

    def rotate(j):
        j = jnp.int32(j)
        s = source(j)
        place = lax.rem(j, BASIS_SLOTS)
        for copy in basis_copies(j):
            copy.wait()
        acc_a[...] += contract_last(qbuf[s, :, :width_a], slot_a[place])
        acc_g[...] += contract_last(qbuf[s, :, width_a:], slot_g[place])

        @pl.when(j + BASIS_SLOTS < n)
        def _():
            for copy in basis_copies(j + BASIS_SLOTS):
                copy.start()

    sent = stage(0, qbuf, rotate)
    bbuf[me, :, :width_a] = acc_a[...].astype(jnp.bfloat16)
    bbuf[me, :, width_a:] = acc_g[...].astype(jnp.bfloat16)

    def project(j):
        s = source(jnp.int32(j))
        cols_a = pl.ds(pl.multiple_of(s * width_a, LANES), width_a)
        cols_g = pl.ds(pl.multiple_of(s * width_g, LANES), width_g)
        proj_a[...] += contract_last(bbuf[s, :, :width_a], acts_v[:, cols_a])
        proj_g[...] += contract_last(bbuf[s, :, width_a:], grads_v[:, cols_g])

    for copy in tokens:
        copy.wait()
    sent += stage(1, bbuf, project)

    queries = scores_ref.shape[0]
    seq_count = scores_ref.shape[1]
    blocks_q, slots_q = cand_ref.shape
    token_sums = (proj_a[...] * proj_g[...]).reshape(queries, rows // queries, -1).sum(axis=1)
    tok_lane = lax.broadcasted_iota(jnp.int32, token_sums.shape, 1)
    lane = lax.broadcasted_iota(jnp.int32, (queries, LANES), 1)
    row = lax.broadcasted_iota(jnp.int32, (queries, LANES), 0)
    tile = jnp.zeros((queries, LANES), jnp.float32)
    for q in range(seq_count):
        inside = (tok_lane >= q * SEQ_LEN) & (tok_lane < (q + 1) * SEQ_LEN)
        total = jnp.sum(jnp.where(inside, token_sums, 0.0), axis=1, keepdims=True)
        tile = jnp.where(lane == q, total, tile)
    masking = jnp.zeros((queries, LANES), jnp.float32)
    per_block = queries // blocks_q
    for b in range(blocks_q):
        named = jnp.float32(0.0)
        for slot in range(slots_q):
            hit = (slot < count_ref[b]) & (cand_ref[b, slot] == me)
            named += jnp.where(hit, 1.0, 0.0)
        chosen = (row >= b * per_block) & (row < (b + 1) * per_block)
        masking = jnp.where(chosen, named, masking)
    tile = tile * masking
    scores_ref[...] = tile[:, :seq_count]
    seq_all[me] = tile

    def score_copy(j, origin):
        return pltpu.make_async_remote_copy(
            src_ref=seq_all.at[origin], dst_ref=seq_all.at[origin],
            send_sem=score_send.at[j], recv_sem=score_land.at[origin],
            device_id={"param": lax.rem(me + j, n)}, device_id_type=pl.DeviceIdType.MESH,
        )

    def give(j, carry):
        score_copy(j, me).start()
        return carry

    def take(j, carry):
        score_copy(j, lax.rem(me + j, n)).wait_recv()
        return carry

    def given(j, carry):
        score_copy(j, me).wait_send()
        return carry

    lax.fori_loop(1, n, give, 0)
    for copy in sent:
        copy.wait_send()
    lax.fori_loop(1, n, take, 0)
    values = jnp.zeros((queries, LANES), jnp.float32)
    for p in range(n):
        part = seq_all[p]
        values += part if p == 0 else pltpu.roll(part, p * seq_count, 1)
    total_seq = n * seq_count
    values = jnp.where(lane < total_seq, values, -jnp.inf)
    rank = jnp.zeros((queries, LANES), jnp.int32)
    for k in range(total_seq):
        rival = values[:, k : k + 1]
        ahead = (rival > values) | ((rival == values) & (lane > k))
        rank += ahead.astype(jnp.int32)
    best = jnp.zeros((queries, LANES), jnp.float32)
    for m in range(TOPK):
        picked = jnp.sum(jnp.where(rank == m, values, 0.0), axis=1, keepdims=True)
        best = jnp.where(lane == m, picked, best)
    top_ref[...] = best[:, :TOPK]
    lax.fori_loop(1, n, given, 0)


def ring_scores(n, basis_a, basis_g, query_a, query_g, acts, grads, cand_blocks, cand_count):
    queries, rank_size, width_a = query_a.shape
    width_g = query_g.shape[2]
    rows = queries * rank_size
    tok_rows = acts.shape[0]
    stride = width_a + width_g
    reach = n // CORES // 2
    anywhere = pl.BlockSpec(memory_space=pl.ANY)
    scalars = pl.BlockSpec(memory_space=pltpu.SMEM)
    whole = pl.BlockSpec(memory_space=pltpu.VMEM)
    dma = pltpu.SemaphoreType.DMA
    flops = 2 * rows * (basis_a.size + basis_g.size + acts.size + grads.size)
    moved = 2 * (basis_a.size + basis_g.size + acts.size + grads.size)
    return pl.pallas_call(
        functools.partial(ring_kernel, n),
        out_shape=(
            jax.ShapeDtypeStruct((queries, tok_rows // SEQ_LEN), jnp.float32),
            jax.ShapeDtypeStruct((queries, TOPK), jnp.float32),
        ),
        in_specs=[anywhere] * 6 + [scalars] * 2,
        out_specs=(whole, whole),
        scratch_shapes=[
            pltpu.VMEM((n, rows, stride), jnp.bfloat16),
            pltpu.VMEM((n, rows, stride), jnp.bfloat16),
            pltpu.VMEM((BASIS_SLOTS, width_a, width_a), jnp.bfloat16),
            pltpu.VMEM((BASIS_SLOTS, width_g, width_g), jnp.bfloat16),
            pltpu.VMEM(acts.shape, jnp.bfloat16),
            pltpu.VMEM(grads.shape, jnp.bfloat16),
            pltpu.VMEM((rows, width_a), jnp.float32),
            pltpu.VMEM((rows, width_g), jnp.float32),
            pltpu.VMEM((rows, tok_rows), jnp.float32),
            pltpu.VMEM((rows, tok_rows), jnp.float32),
            pltpu.VMEM((n, queries, LANES), jnp.float32),
            dma((2,)),
            dma((2, BASIS_SLOTS)),
            dma((2,)),
            dma((2, reach, 2)),
            dma((2, reach, 2)),
            dma((2, 2, reach + 1, 2)),
            dma((2, n, 2)),
            dma((n,)),
            dma((n,)),
        ],
        compiler_params=pltpu.CompilerParams(
            collective_id=0, has_side_effects=True, vmem_limit_bytes=56 * 1024 * 1024
        ),
        cost_estimate=pl.CostEstimate(flops=flops, bytes_accessed=moved, transcendentals=0),
    )(
        query_a.reshape(rows, width_a), query_g.reshape(rows, width_g),
        basis_a, basis_g, acts, grads, cand_blocks, cand_count,
    )


def plain_scores(basis_a, basis_g, query_a, query_g, acts, grads, cand_blocks, cand_count):
    queries, rank_size, width_a = query_a.shape
    width_g = query_g.shape[2]
    rows = queries * rank_size
    stride = width_a + width_g
    tok_rows = acts.shape[0]
    seq_count = tok_rows // SEQ_LEN
    per_block = queries // cand_blocks.shape[0]
    my_index = lax.axis_index("param")

    def whole(part_a, part_g):
        joined = jnp.concatenate([part_a, part_g], axis=1)
        piece = lax.all_gather(joined, "param", axis=1, tiled=True)
        divided = piece.reshape(rows, -1, stride)
        return (
            divided[:, :, :width_a].reshape(rows, -1),
            divided[:, :, width_a:].reshape(rows, -1),
        )

    full_a, full_g = whole(query_a.reshape(rows, width_a), query_g.reshape(rows, width_g))
    back_a = contract_last(full_a, basis_a).astype(jnp.bfloat16)
    back_g = contract_last(full_g, basis_g).astype(jnp.bfloat16)
    full_a, full_g = whole(back_a, back_g)
    products = contract_last(full_a, acts) * contract_last(full_g, grads)
    seq_sums = products.reshape(queries, rank_size, seq_count, SEQ_LEN).sum(axis=(1, 3))
    positions = jnp.arange(cand_blocks.shape[1], dtype=jnp.int32)
    live_slot = positions[None, :] < cand_count[:, None]
    named = jnp.sum((live_slot & (cand_blocks == my_index)).astype(jnp.float32), axis=1)
    scores = seq_sums * jnp.repeat(named, per_block)[:, None]
    every = lax.all_gather(scores, "param", axis=1, tiled=True)
    return scores, lax.top_k(every, TOPK)[0]


def solution(mesh):
    n = mesh.shape["param"]

    def shards(basis_a, basis_g, query_a, query_g, acts, grads, cand_blocks, cand_count):
        args = (basis_a, basis_g, query_a, query_g, acts, grads, cand_blocks, cand_count)
        fits = (
            n % (2 * CORES * X_CHIPS) == 0
            and query_a.shape[2] % LANES == 0
            and query_g.shape[2] % LANES == 0
            and n * (acts.shape[0] // SEQ_LEN) <= LANES
        )
        return ring_scores(n, *args) if fits else plain_scores(*args)

    in_specs = (
        P("param", None),
        P("param", None),
        P("grp", None, "param"),
        P("grp", None, "param"),
        P(("grp", "param"), None),
        P(("grp", "param"), None),
        P("grp", None),
        P("grp"),
    )
    out_specs = (P("grp", "param"), P("grp", None))
    return jax.shard_map(shards, mesh=mesh, in_specs=in_specs, out_specs=out_specs, check_vma=False)
```

time: 341 us -> 135 us (0.40)
  waiting for transfers between devices: 190 us -> 0 us
  Pallas kernels: 0 us -> 132 us
  local copies, waits for them, and re-layouts: 69.7 us -> 2.59 us
  matrix products: 29.7 us -> 0 us
  blocking collectives: 18.8 us -> 0 us
  other arithmetic: 17.9 us -> 0 us
  between operations: 14.2 us -> 0.64 us
    all_gather x2 -> x0, waiting for transfers between devices: 190 us -> none  [the longest x1 97.5 us: shards(): piece = lax.all_gather(joined, 'param', axis=2, tiled=True)]
    pallas_call x0 -> x1, Pallas kernels: none -> 132 us  [ring_scores(): pl.pallas_call(functools.partial(ring_kernel, n), out_shape=(jax.ShapeDty...]
    unnamed x22 -> x1, local copies, waits for them, and re-layouts: 50.3 us -> 1.26 us
    dot_general x4 -> x0, matrix products: 29.7 us -> none  [contract_last(): lax.dot_general(left, right, (((1,), (1,)), ((), ())), preferred_element_...]
    all_gather x1 -> x0, blocking collectives: 18.8 us -> none  [merged(): gathered = lax.all_gather(part, axis)]
    slice x4 -> x0, local copies, waits for them, and re-layouts: 15.6 us -> none  [the longest x2 10.3 us: shards(): part_g = divided[:, :, width_a:].reshape(rows_qr, shard_count * width_g)]
    top_k x16 -> x0, other arithmetic: 13.3 us -> none  [the longest x15 12.5 us: top_values(): return lax.top_k(jnp.concatenate([first_set, second_set], axis=1), TOPK)[0]]
    concatenate x17 -> x0, other arithmetic: 4.23 us -> none  [the longest x1 2.16 us: shards(): joined = jnp.concatenate([query_a, query_g], axis=2)]
  transfers between devices with their start and end apart: 2 -> 0, of which waited for: 2 -> 0; matrix products, arithmetic and copies ran while one was open for 0% -> 0% of each run, Pallas kernels for 0% -> 0%
where the time goes in v1:
time: 135 us
  Pallas kernels  132 us (98%)
  local copies, waits for them, and re-layouts  2.59 us (2%)
    pallas_call x1, Pallas kernels, ring_scores(): pl.pallas_call(functools.partial(ring_kernel, n), out_shape=(jax.ShapeDty...  132 us

profile of v1, /device:TPU:0, one launch (start us, length us, event | category | flops | bytes accessed | tf_op | source)
XLA Modules:
  0.0 134.7 jit_solution(12859472920407973811)
XLA Ops:
  0.6 131.5 %shard_map.95 = (f32[8,3]{1,0:T(8,128)}, f32[8,16]{1,0:T(8,128)}) custom-call(bf16[256,512]{1,0:T(8,128)(2,1)} %bitcast.3, bf16[256,896]{1,0:T(8,128)(2,1)} %bitcast.2, bf16[512,8192]{1,0:T(8,128)(2,1)} %ba_ref.1, bf16[896,14336]{1,0:T(8,128)(2,1)} %bg_ref.1, bf16[192,8192]{1,0:T(8,128)(2,1)} %acts_ref.1, bf16[192,14336]{1,0:T(8,128)(2,1)} %grads_ref.1, ...), custom_call_target="tpu_custom_call" | custom-call | flops 10938744832 | bytes 42729472 | tf_op jit(solution)/shard_map/pallas_call | solution.py:272
  132.2 1.3 copy.10
  133.5 1.3 copy.12

commit v2 on v1

--- a/solution.py
+++ b/solution.py
@@ -23,8 +23,9 @@
 
 def ring_kernel(
     n, qa_ref, qg_ref, ba_ref, bg_ref, acts_ref, grads_ref, cand_ref, count_ref,
-    scores_ref, top_ref,
-    qbuf, bbuf, slot_a, slot_g, acts_v, grads_v, acc_a, acc_g, proj_a, proj_g, seq_all,
+    out_ref,
+    qa_all, qg_all, ba_all, bg_all, slot_a, slot_g, acts_v, grads_v,
+    acc_a, acc_g, proj_a, proj_g, seq_all,
     own_sem, basis_sem, token_sem,
     right_sem, left_sem, pair_sem, land_sem, score_send, score_land,
 ):
@@ -59,19 +60,17 @@
         side = lax.div(t, 2)
         return holder(pos - k + 2 * k * side, core + flip * (1 - 2 * core))
 
-    def basis_copies(j):
-        s = source(j)
+    def basis_copy(part, j):
+        basis_ref, slots, width = ((ba_ref, slot_a, width_a), (bg_ref, slot_g, width_g))[part]
         place = lax.rem(j, BASIS_SLOTS)
-        cols_a = pl.ds(pl.multiple_of(s * width_a, LANES), width_a)
-        cols_g = pl.ds(pl.multiple_of(s * width_g, LANES), width_g)
-        return (
-            pltpu.make_async_copy(ba_ref.at[:, cols_a], slot_a.at[place], basis_sem.at[0, place]),
-            pltpu.make_async_copy(bg_ref.at[:, cols_g], slot_g.at[place], basis_sem.at[1, place]),
+        cols = pl.ds(pl.multiple_of(source(j) * width, LANES), width)
+        return pltpu.make_async_copy(
+            basis_ref.at[:, cols], slots.at[place], basis_sem.at[part, place]
         )
 
     own = (
-        pltpu.make_async_copy(qa_ref, qbuf.at[me, :, pl.ds(0, width_a)], own_sem.at[0]),
-        pltpu.make_async_copy(qg_ref, qbuf.at[me, :, pl.ds(width_a, width_g)], own_sem.at[1]),
+        pltpu.make_async_copy(qa_ref, qa_all.at[me], own_sem.at[0]),
+        pltpu.make_async_copy(qg_ref, qg_all.at[me], own_sem.at[1]),
     )
     tokens = (
         pltpu.make_async_copy(acts_ref, acts_v, token_sem.at[0]),
@@ -79,11 +78,6 @@
     )
     for copy in own:
         copy.start()
-    for j in range(BASIS_SLOTS):
-        for copy in basis_copies(jnp.int32(j)):
-            copy.start()
-    for copy in tokens:
-        copy.start()
 
     barrier = pltpu.get_barrier_semaphore()
 
@@ -95,17 +89,18 @@
         return carry
 
     lax.fori_loop(1, n, greet, 0)
-    acc_a[...] = jnp.zeros_like(acc_a)
-    acc_g[...] = jnp.zeros_like(acc_g)
-    proj_a[...] = jnp.zeros_like(proj_a)
-    proj_g[...] = jnp.zeros_like(proj_g)
+    for j in range(BASIS_SLOTS):
+        for part in (0, 1):
+            basis_copy(part, jnp.int32(j)).start()
+    for copy in tokens:
+        copy.start()
+    for total in (acc_a, acc_g, proj_a, proj_g):
+        total[...] = jnp.zeros_like(total)
     pl.semaphore_wait(barrier, n - 1)
-    for copy in own:
-        copy.wait()
-
-    def stage(number, buf, compute):
-        sent = []
-
+
+    sent = []
+
+    def gather(number, buf, compute):
         def push(s, h, target, sem):
             view = buf.at[s, pl.ds(h * half, half), :]
             return pltpu.make_async_remote_copy(
@@ -121,18 +116,20 @@
         def landed(s, h):
             push(s, h, pair, pair_sem.at[number, 0, 0, h]).wait_recv()
 
-        for h in (0, 1):
-            send(me, h, right, right_sem.at[number, 0, h])
-            send(me, 1 - h, left, left_sem.at[number, 0, 1 - h])
-        for h in (0, 1):
-            send(me, h, pair, pair_sem.at[number, 0, 0, h])
-        compute(0)
-        for h in (0, 1):
-            landed(pair, h)
-        compute(1)
-        for k in range(1, reach):
+        def begin():
+            for h in (0, 1):
+                send(me, h, right, right_sem.at[number, 0, h])
+                send(me, 1 - h, left, left_sem.at[number, 0, 1 - h])
+            for h in (0, 1):
+                send(me, h, pair, pair_sem.at[number, 0, 0, h])
+
+        def forward(k):
             back, front = holder(pos - k, core), holder(pos + k, core)
             for h in (0, 1):
+                if k == reach:
+                    landed(back, h)
+                    send(back, h, pair, pair_sem.at[number, 0, k, h])
+                    continue
                 landed(back, h)
                 if k < reach - 1 or h == 0:
                     send(back, h, right, right_sem.at[number, k, h])
@@ -141,6 +138,15 @@
                     send(front, 1 - h, left, left_sem.at[number, k, 1 - h])
                 send(back, h, pair, pair_sem.at[number, 0, k, h])
                 send(front, 1 - h, pair, pair_sem.at[number, 1, k, 1 - h])
+
+        def work(k):
+            if k in (0, reach):
+                first = 0 if k == 0 else n - 2
+                compute(jnp.int32(first))
+                for h in (0, 1):
+                    landed(holder(pos - k, 1 - core), h)
+                compute(jnp.int32(first + 1))
+                return
             for other in (holder(pos - k, 1 - core), holder(pos + k, 1 - core)):
                 for h in (0, 1):
                     landed(other, h)
@@ -150,47 +156,86 @@
                 return carry
 
             lax.fori_loop(4 * k - 2, 4 * k + 2, body, 0)
-        far = holder(pos - reach, core)
-        for h in (0, 1):
-            landed(far, h)
-            send(far, h, pair, pair_sem.at[number, 0, reach, h])
-        compute(n - 2)
-        for h in (0, 1):
-            landed(holder(pos - reach, 1 - core), h)
-        compute(n - 1)
-        return sent
-
-    def rotate(j):
-        j = jnp.int32(j)
-        s = source(j)
-        place = lax.rem(j, BASIS_SLOTS)
-        for copy in basis_copies(j):
-            copy.wait()
-        acc_a[...] += contract_last(qbuf[s, :, :width_a], slot_a[place])
-        acc_g[...] += contract_last(qbuf[s, :, width_a:], slot_g[place])
-
-        @pl.when(j + BASIS_SLOTS < n)
-        def _():
-            for copy in basis_copies(j + BASIS_SLOTS):
-                copy.start()
-
-    sent = stage(0, qbuf, rotate)
-    bbuf[me, :, :width_a] = acc_a[...].astype(jnp.bfloat16)
-    bbuf[me, :, width_a:] = acc_g[...].astype(jnp.bfloat16)
-
-    def project(j):
-        s = source(jnp.int32(j))
-        cols_a = pl.ds(pl.multiple_of(s * width_a, LANES), width_a)
-        cols_g = pl.ds(pl.multiple_of(s * width_g, LANES), width_g)
-        proj_a[...] += contract_last(bbuf[s, :, :width_a], acts_v[:, cols_a])
-        proj_g[...] += contract_last(bbuf[s, :, width_a:], grads_v[:, cols_g])
-
+
+        return begin, forward, work
+
+    def rotate(part, query, slots, total):
+        def compute(j):
+            place = lax.rem(j, BASIS_SLOTS)
+            basis_copy(part, j).wait()
+            total[...] += contract_last(query[source(j)], slots[place])
+
+            @pl.when(j + BASIS_SLOTS < n)
+            def _():
+                basis_copy(part, j + BASIS_SLOTS).start()
+
+        return compute
+
+    def project(backs, held, width, total):
+        def compute(j):
+            s = source(j)
+            cols = pl.ds(pl.multiple_of(s * width, LANES), width)
+            total[...] += contract_last(backs[s], held[:, cols])
+
+        return compute
+
+    begin_qa, forward_qa, work_qa = gather(0, qa_all, rotate(0, qa_all, slot_a, acc_a))
+    begin_qg, forward_qg, work_qg = gather(1, qg_all, rotate(1, qg_all, slot_g, acc_g))
+    begin_ba, forward_ba, work_ba = gather(2, ba_all, project(ba_all, acts_v, width_a, proj_a))
+    begin_bg, forward_bg, work_bg = gather(3, bg_all, project(bg_all, grads_v, width_g, proj_g))
+    last = reach - 1
+
+    own[0].wait()
+    begin_qa()
+    own[1].wait()
+    work_qa(0)
+    forward_qa(1)
+    begin_qg()
+    work_qa(1)
+    work_qg(0)
+    for k in range(2, last):
+        forward_qa(k)
+        work_qa(k)
+        forward_qg(k - 1)
+        work_qg(k - 1)
+    forward_qa(last)
+    forward_qg(last - 1)
+    work_qa(last)
+    forward_qa(reach)
+    work_qa(reach)
+    ba_all[me] = acc_a[...].astype(jnp.bfloat16)
+    begin_ba()
+    work_qg(last - 1)
+    forward_qg(last)
     for copy in tokens:
         copy.wait()
-    sent += stage(1, bbuf, project)
-
-    queries = scores_ref.shape[0]
-    seq_count = scores_ref.shape[1]
+    work_ba(0)
+    work_qg(last)
+    forward_ba(1)
+    forward_qg(reach)
+    work_qg(reach)
+    bg_all[me] = acc_g[...].astype(jnp.bfloat16)
+    begin_bg()
+    work_ba(1)
+    work_bg(0)
+    for k in range(2, last):
+        forward_ba(k)
+        work_ba(k)
+        forward_bg(k - 1)
+        work_bg(k - 1)
+    forward_ba(last)
+    forward_bg(last - 1)
+    work_ba(last)
+    forward_ba(reach)
+    work_ba(reach)
+    work_bg(last - 1)
+    forward_bg(last)
+    work_bg(last)
+    forward_bg(reach)
+    work_bg(reach)
+
+    queries = seq_all.shape[1]
+    seq_count = acts_v.shape[0] // SEQ_LEN
     blocks_q, slots_q = cand_ref.shape
     token_sums = (proj_a[...] * proj_g[...]).reshape(queries, rows // queries, -1).sum(axis=1)
     tok_lane = lax.broadcasted_iota(jnp.int32, token_sums.shape, 1)
@@ -211,7 +256,6 @@
         chosen = (row >= b * per_block) & (row < (b + 1) * per_block)
         masking = jnp.where(chosen, named, masking)
     tile = tile * masking
-    scores_ref[...] = tile[:, :seq_count]
     seq_all[me] = tile
 
     def score_copy(j, origin):
@@ -234,6 +278,7 @@
         return carry
 
     lax.fori_loop(1, n, give, 0)
+    out_ref[:queries, :] = tile
     for copy in sent:
         copy.wait_send()
     lax.fori_loop(1, n, take, 0)
@@ -241,8 +286,15 @@
     for p in range(n):
         part = seq_all[p]
         values += part if p == 0 else pltpu.roll(part, p * seq_count, 1)
-    total_seq = n * seq_count
-    values = jnp.where(lane < total_seq, values, -jnp.inf)
+    out_ref[queries:, :] = values
+    lax.fori_loop(1, n, given, 0)
+
+
+def rank_kernel(total_seq, in_ref, scores_ref, top_ref):
+    queries, seq_count = scores_ref.shape
+    scores_ref[...] = in_ref[:queries, :seq_count]
+    lane = lax.broadcasted_iota(jnp.int32, (queries, LANES), 1)
+    values = jnp.where(lane < total_seq, in_ref[queries:, :], -jnp.inf)
     rank = jnp.zeros((queries, LANES), jnp.int32)
     for k in range(total_seq):
         rival = values[:, k : k + 1]
@@ -253,7 +305,6 @@
         picked = jnp.sum(jnp.where(rank == m, values, 0.0), axis=1, keepdims=True)
         best = jnp.where(lane == m, picked, best)
     top_ref[...] = best[:, :TOPK]
-    lax.fori_loop(1, n, given, 0)
 
 
 def ring_scores(n, basis_a, basis_g, query_a, query_g, acts, grads, cand_blocks, cand_count):
@@ -261,7 +312,6 @@
     width_g = query_g.shape[2]
     rows = queries * rank_size
     tok_rows = acts.shape[0]
-    stride = width_a + width_g
     reach = n // CORES // 2
     anywhere = pl.BlockSpec(memory_space=pl.ANY)
     scalars = pl.BlockSpec(memory_space=pltpu.SMEM)
@@ -269,17 +319,17 @@
     dma = pltpu.SemaphoreType.DMA
     flops = 2 * rows * (basis_a.size + basis_g.size + acts.size + grads.size)
     moved = 2 * (basis_a.size + basis_g.size + acts.size + grads.size)
-    return pl.pallas_call(
+    seq_count = tok_rows // SEQ_LEN
+    gathered = pl.pallas_call(
         functools.partial(ring_kernel, n),
-        out_shape=(
-            jax.ShapeDtypeStruct((queries, tok_rows // SEQ_LEN), jnp.float32),
-            jax.ShapeDtypeStruct((queries, TOPK), jnp.float32),
-        ),
+        out_shape=jax.ShapeDtypeStruct((2 * queries, LANES), jnp.float32),
         in_specs=[anywhere] * 6 + [scalars] * 2,
-        out_specs=(whole, whole),
+        out_specs=whole,
         scratch_shapes=[
-            pltpu.VMEM((n, rows, stride), jnp.bfloat16),
-            pltpu.VMEM((n, rows, stride), jnp.bfloat16),
+            pltpu.VMEM((n, rows, width_a), jnp.bfloat16),
+            pltpu.VMEM((n, rows, width_g), jnp.bfloat16),
+            pltpu.VMEM((n, rows, width_a), jnp.bfloat16),
+            pltpu.VMEM((n, rows, width_g), jnp.bfloat16),
             pltpu.VMEM((BASIS_SLOTS, width_a, width_a), jnp.bfloat16),
             pltpu.VMEM((BASIS_SLOTS, width_g, width_g), jnp.bfloat16),
             pltpu.VMEM(acts.shape, jnp.bfloat16),
@@ -292,10 +342,10 @@
             dma((2,)),
             dma((2, BASIS_SLOTS)),
             dma((2,)),
-            dma((2, reach, 2)),
-            dma((2, reach, 2)),
-            dma((2, 2, reach + 1, 2)),
-            dma((2, n, 2)),
+            dma((4, reach, 2)),
+            dma((4, reach, 2)),
+            dma((4, 2, reach + 1, 2)),
+            dma((4, n, 2)),
             dma((n,)),
             dma((n,)),
         ],
@@ -307,6 +357,15 @@
         query_a.reshape(rows, width_a), query_g.reshape(rows, width_g),
         basis_a, basis_g, acts, grads, cand_blocks, cand_count,
     )
+    return pl.pallas_call(
+        functools.partial(rank_kernel, n * seq_count),
+        out_shape=(
+            jax.ShapeDtypeStruct((queries, seq_count), jnp.float32),
+            jax.ShapeDtypeStruct((queries, TOPK), jnp.float32),
+        ),
+        in_specs=[whole],
+        out_specs=(whole, whole),
+    )(gathered)
 
 
 def plain_scores(basis_a, basis_g, query_a, query_g, acts, grads, cand_blocks, cand_count):
@@ -349,6 +408,7 @@
         args = (basis_a, basis_g, query_a, query_g, acts, grads, cand_blocks, cand_count)
         fits = (
             n % (2 * CORES * X_CHIPS) == 0
+            and n >= 8 * CORES
             and query_a.shape[2] % LANES == 0
             and query_g.shape[2] % LANES == 0
             and n * (acts.shape[0] // SEQ_LEN) <= LANES

time: 135 us -> 129 us (0.956)
  Pallas kernels: 132 us -> 127 us
    pallas_call x1 -> x2, Pallas kernels: 132 us -> 127 us  [the longest x1 125 us: ring_scores(): pl.pallas_call(functools.partial(ring_kernel, n), out_shape=jax.ShapeDtyp...]
where the time goes in v2:
time: 129 us
  Pallas kernels  127 us (98%)
  local copies, waits for them, and re-layouts  1.32 us (1%)
    pallas_call x1, Pallas kernels, ring_scores(): pl.pallas_call(functools.partial(ring_kernel, n), out_shape=jax.ShapeDtyp...  125 us

profile of v2, /device:TPU:0, one launch (start us, length us, event | category | flops | bytes accessed | tf_op | source)
XLA Modules:
  0.0 128.8 jit_solution(12331090787528756359)
XLA Ops:
  0.6 125.3 %shard_map.95.in_ref = f32[16,128]{1,0:T(8,128)} custom-call(bf16[256,512]{1,0:T(8,128)(2,1)} %bitcast.3, bf16[256,896]{1,0:T(8,128)(2,1)} %bitcast.2, bf16[512,8192]{1,0:T(8,128)(2,1)} %ba_ref.1, bf16[896,14336]{1,0:T(8,128)(2,1)} %bg_ref.1, bf16[192,8192]{1,0:T(8,128)(2,1)} %acts_ref.1, bf16[192,14336]{1,0:T(8,128)(2,1)} %grads_ref.1, s32[4,4]{1,0:T(4,128)} %cand_ref.1, ...), custom_call_target="tpu_custom_call" | custom-call | flops 10938744832 | bytes 42729472 | tf_op jit(solution)/shard_map/pallas_call | solution.py:323
  126.0 1.5 %shard_map.96 = (f32[8,3]{1,0:T(8,128)}, f32[8,16]{1,0:T(8,128)}) custom-call(f32[16,128]{1,0:T(8,128)} %shard_map.95.in_ref), custom_call_target="tpu_custom_call" | custom-call | tf_op jit(solution)/shard_map/pallas_call | solution.py:360
  127.5 1.3 %copy.10 = f32[8,3]{0,1:T(4,128)} copy(f32[8,3]{1,0:T(8,128)} %get-tuple-element.2) | data formatting | bytes 192 | tf_op jit(solution)/shard_map/pallas_call | solution.py:360

commit v3 on v2

--- a/solution.py
+++ b/solution.py
@@ -25,9 +25,9 @@
     n, qa_ref, qg_ref, ba_ref, bg_ref, acts_ref, grads_ref, cand_ref, count_ref,
     out_ref,
     qa_all, qg_all, ba_all, bg_all, slot_a, slot_g, acts_v, grads_v,
-    acc_a, acc_g, proj_a, proj_g, seq_all,
+    acc_a, acc_g, proj_a, proj_g, plane_all, line_all,
     own_sem, basis_sem, token_sem,
-    right_sem, left_sem, pair_sem, land_sem, score_send, score_land,
+    right_sem, left_sem, pair_sem, land_sem, plane_send, plane_land, line_send, line_land,
 ):
     rows, width_a = qa_ref.shape
     width_g = qg_ref.shape[1]
@@ -49,6 +49,15 @@
         z = place + x * (chips - 1 - 2 * place)
         return (z * X_CHIPS + x) * CORES + which
 
+    plane = X_CHIPS * CORES
+    seat = lax.rem(me, plane)
+
+    def plane_peer(j):
+        return z_pos * plane + lax.rem(seat + j, plane)
+
+    def line_peer(j):
+        return lax.rem(z_pos + j, z_chips) * plane + seat
+
     right = holder(pos + 1, core)
     left = holder(pos - 1, core)
 
@@ -81,14 +90,12 @@
 
     barrier = pltpu.get_barrier_semaphore()
 
-    def greet(j, carry):
-        pl.semaphore_signal(
-            barrier, inc=1, device_id={"param": lax.rem(me + j, n)},
-            device_id_type=pl.DeviceIdType.MESH,
-        )
-        return carry
-
-    lax.fori_loop(1, n, greet, 0)
+    for peer, count in ((plane_peer, plane), (line_peer, z_chips)):
+        for j in range(1, count):
+            pl.semaphore_signal(
+                barrier, inc=1, device_id={"param": peer(j)},
+                device_id_type=pl.DeviceIdType.MESH,
+            )
     for j in range(BASIS_SLOTS):
         for part in (0, 1):
             basis_copy(part, jnp.int32(j)).start()
@@ -96,7 +103,7 @@
         copy.start()
     for total in (acc_a, acc_g, proj_a, proj_g):
         total[...] = jnp.zeros_like(total)
-    pl.semaphore_wait(barrier, n - 1)
+    pl.semaphore_wait(barrier, plane + z_chips - 2)
 
     sent = []
 
@@ -229,12 +236,15 @@
     forward_ba(reach)
     work_ba(reach)
     work_bg(last - 1)
+    settled = len(sent)
     forward_bg(last)
     work_bg(last)
+    for copy in sent[:settled]:
+        copy.wait_send()
     forward_bg(reach)
     work_bg(reach)
 
-    queries = seq_all.shape[1]
+    queries = plane_all.shape[1]
     seq_count = acts_v.shape[0] // SEQ_LEN
     blocks_q, slots_q = cand_ref.shape
     token_sums = (proj_a[...] * proj_g[...]).reshape(queries, rows // queries, -1).sum(axis=1)
@@ -256,43 +266,46 @@
         chosen = (row >= b * per_block) & (row < (b + 1) * per_block)
         masking = jnp.where(chosen, named, masking)
     tile = tile * masking
-    seq_all[me] = tile
-
-    def score_copy(j, origin):
-        return pltpu.make_async_remote_copy(
-            src_ref=seq_all.at[origin], dst_ref=seq_all.at[origin],
-            send_sem=score_send.at[j], recv_sem=score_land.at[origin],
-            device_id={"param": lax.rem(me + j, n)}, device_id_type=pl.DeviceIdType.MESH,
-        )
-
-    def give(j, carry):
-        score_copy(j, me).start()
-        return carry
-
-    def take(j, carry):
-        score_copy(j, lax.rem(me + j, n)).wait_recv()
-        return carry
-
-    def given(j, carry):
-        score_copy(j, me).wait_send()
-        return carry
-
-    lax.fori_loop(1, n, give, 0)
     out_ref[:queries, :] = tile
-    for copy in sent:
+
+    def exchange(everyone, mine, count, peer, send_sem, recv_sem, step):
+        copies = []
+        for j in range(1, count):
+            copy = pltpu.make_async_remote_copy(
+                src_ref=everyone.at[mine], dst_ref=everyone.at[mine],
+                send_sem=send_sem.at[j], recv_sem=recv_sem.at[mine],
+                device_id={"param": peer(j)}, device_id_type=pl.DeviceIdType.MESH,
+            )
+            copy.start()
+            copies.append(copy)
+        for j in range(1, count):
+            origin = lax.rem(mine + j, count)
+            pltpu.make_async_remote_copy(
+                src_ref=everyone.at[origin], dst_ref=everyone.at[origin],
+                send_sem=send_sem.at[j], recv_sem=recv_sem.at[origin],
+                device_id={"param": peer(j)}, device_id_type=pl.DeviceIdType.MESH,
+            ).wait_recv()
+        merged = everyone[0]
+        for p in range(1, count):
+            merged += pltpu.roll(everyone[p], p * step, 1)
+        return merged, copies
+
+    plane_all[seat] = tile
+    merged, plane_sent = exchange(
+        plane_all, seat, plane, plane_peer, plane_send, plane_land, seq_count
+    )
+    line_all[z_pos] = merged
+    merged, line_sent = exchange(
+        line_all, z_pos, z_chips, line_peer, line_send, line_land, plane * seq_count
+    )
+    out_ref[queries:, :] = merged
+    for copy in sent[settled:] + plane_sent + line_sent:
         copy.wait_send()
-    lax.fori_loop(1, n, take, 0)
-    values = jnp.zeros((queries, LANES), jnp.float32)
-    for p in range(n):
-        part = seq_all[p]
-        values += part if p == 0 else pltpu.roll(part, p * seq_count, 1)
-    out_ref[queries:, :] = values
-    lax.fori_loop(1, n, given, 0)
 
 
 def rank_kernel(total_seq, in_ref, scores_ref, top_ref):
-    queries, seq_count = scores_ref.shape
-    scores_ref[...] = in_ref[:queries, :seq_count]
+    seq_count, queries = scores_ref.shape
+    scores_ref[...] = in_ref[:queries, :].T[:seq_count, :]
     lane = lax.broadcasted_iota(jnp.int32, (queries, LANES), 1)
     values = jnp.where(lane < total_seq, in_ref[queries:, :], -jnp.inf)
     rank = jnp.zeros((queries, LANES), jnp.int32)
@@ -320,6 +333,7 @@
     flops = 2 * rows * (basis_a.size + basis_g.size + acts.size + grads.size)
     moved = 2 * (basis_a.size + basis_g.size + acts.size + grads.size)
     seq_count = tok_rows // SEQ_LEN
+    plane = X_CHIPS * CORES
     gathered = pl.pallas_call(
         functools.partial(ring_kernel, n),
         out_shape=jax.ShapeDtypeStruct((2 * queries, LANES), jnp.float32),
@@ -338,7 +352,8 @@
             pltpu.VMEM((rows, width_g), jnp.float32),
             pltpu.VMEM((rows, tok_rows), jnp.float32),
             pltpu.VMEM((rows, tok_rows), jnp.float32),
-            pltpu.VMEM((n, queries, LANES), jnp.float32),
+            pltpu.VMEM((plane, queries, LANES), jnp.float32),
+            pltpu.VMEM((n // plane, queries, LANES), jnp.float32),
             dma((2,)),
             dma((2, BASIS_SLOTS)),
             dma((2,)),
@@ -346,8 +361,10 @@
             dma((4, reach, 2)),
             dma((4, 2, reach + 1, 2)),
             dma((4, n, 2)),
-            dma((n,)),
-            dma((n,)),
+            dma((plane,)),
+            dma((plane,)),
+            dma((n // plane,)),
+            dma((n // plane,)),
         ],
         compiler_params=pltpu.CompilerParams(
             collective_id=0, has_side_effects=True, vmem_limit_bytes=56 * 1024 * 1024
@@ -357,15 +374,16 @@
         query_a.reshape(rows, width_a), query_g.reshape(rows, width_g),
         basis_a, basis_g, acts, grads, cand_blocks, cand_count,
     )
-    return pl.pallas_call(
+    scores, top_scores = pl.pallas_call(
         functools.partial(rank_kernel, n * seq_count),
         out_shape=(
-            jax.ShapeDtypeStruct((queries, seq_count), jnp.float32),
+            jax.ShapeDtypeStruct((seq_count, queries), jnp.float32),
             jax.ShapeDtypeStruct((queries, TOPK), jnp.float32),
         ),
         in_specs=[whole],
         out_specs=(whole, whole),
     )(gathered)
+    return scores.T, top_scores
 
 
 def plain_scores(basis_a, basis_g, query_a, query_g, acts, grads, cand_blocks, cand_count):

time: 129 us -> 129 us (level)
  local copies, waits for them, and re-layouts: 1.32 us -> 0 us
    pallas_call x1, Pallas kernels: 125 us -> 127 us  [ring_scores(): pl.pallas_call(functools.partial(ring_kernel, n), out_shape=jax.ShapeDtyp...]
    pallas_call x1 -> x0, local copies, waits for them, and re-layouts: 1.32 us -> none  [ring_scores(): pl.pallas_call(functools.partial(rank_kernel, n * seq_count), out_shape=(...]
where the time goes in v3:
time: 129 us
  Pallas kernels  128 us (99%)
    pallas_call x1, Pallas kernels, ring_scores(): pl.pallas_call(functools.partial(ring_kernel, n), out_shape=jax.ShapeDtyp...  127 us

profile of v3, /device:TPU:0, one launch (start us, length us, event | category | flops | bytes accessed | tf_op | source)
XLA Modules:
  0.0 128.9 jit_solution(376856149308479203)
XLA Ops:
  0.6 126.7 %shard_map.95.in_ref = f32[16,128]{1,0:T(8,128)} custom-call(bf16[256,512]{1,0:T(8,128)(2,1)} %bitcast.4, bf16[256,896]{1,0:T(8,128)(2,1)} %bitcast.3, bf16[512,8192]{1,0:T(8,128)(2,1)} %ba_ref.1, bf16[896,14336]{1,0:T(8,128)(2,1)} %bg_ref.1, bf16[192,8192]{1,0:T(8,128)(2,1)} %acts_ref.1, bf16[192,14336]{1,0:T(8,128)(2,1)} %grads_ref.1, s32[4,4]{1,0:T(4,128)} %cand_ref.1, ...), custom_call_target="tpu_custom_call" | custom-call | flops 10938744832 | bytes 42729472 | tf_op jit(solution)/shard_map/pallas_call | solution.py:337
  127.4 1.5 %shard_map.96 = (f32[3,8]{1,0:T(4,128)}, f32[8,16]{1,0:T(8,128)}) custom-call(f32[16,128]{1,0:T(8,128)} %shard_map.95.in_ref), custom_call_target="tpu_custom_call" | custom-call | tf_op jit(solution)/shard_map/pallas_call | solution.py:377
